TPU v7x, 32 devices: a whole 2x2x4 slice. The times are simulated.
32 devices in a mesh: groups: 2 (over x), expert: 16 (over z, y, core).
Axes of the slice: x: 2, y: 2, z: 4, core: 2. Of those that a mesh axis runs over, the one named last changes fastest.
Arguments:
- tokens: bfloat16 [4096, 7168], P(('groups', 'expert')), parts along dimension 0, may hold values from -6 to 6
- out_grad: bfloat16 [4096, 7168], P(('groups', 'expert')), parts along dimension 0, may hold values from -6 to 6
- expert_ids: int32 [4096, 8], P(('groups', 'expert')), parts along dimension 0, may hold values from 0 to 255, as said below
- gate_weights: float32 [4096, 8], P(('groups', 'expert')), parts along dimension 0, may hold values from 0.05 to 1
- w_gate: bfloat16 [16, 7168, 256], P('expert'), may hold values from -0.0625 to 0.0625
- w_up: bfloat16 [16, 7168, 256], P('expert'), may hold values from -0.0625 to 0.0625
- in_proj: bfloat16 [16, 256, 64], P('expert'), may hold values from -0.125 to 0.125
- out_proj: bfloat16 [7168, 64], replicated, may hold values from -0.0625 to 0.0625
Outputs:
- example_grads: float32 [256, 256], P(('groups', 'expert')), parts along dimension 0
There are 2 independent parts, one for each index of `groups`. A program takes and returns all parts, laid end to end along the dimension named above; an argument that names none is the same for every part. Nothing has to cross between parts.
Inputs may be any that keep to these rules, and one draw needn't show every extreme that they name: `expert_ids`: each row names 8 different experts. Among the 128 rows of one device every expert is named by 8, 4 or 2 rows (a quarter, a quarter and a half of the experts); one expert below 2 is named by 8 rows of every device.
All inputs are finite; a program needn't handle non-finite values.
Results may differ from a plain program's by a relative error of at most 0.0041.
Values may be sent and summed in bfloat16 or wider, within the bound.
A program may use at most 128 MiB of HBM per device.

v0:
```python
import jax
import jax.numpy as jnp
from jax import lax
from jax.sharding import PartitionSpec as P

STRIPES = 8
EX_LEN = 512
CAPACITY = 8


def partner(shard, axis, bit):
    return lax.ppermute(shard, axis, [(i, i ^ 1 << bit) for i in range(lax.axis_size(axis))])


def on_device(tokens, out_grad, expert_ids, gate_weights, w_gate, w_up, in_proj, out_proj):
    devices = lax.axis_size("expert")
    flight = devices // STRIPES
    tok_rows = tokens.shape[0]
    width = tokens.shape[1]
    rank_width = out_proj.shape[1]
    capacity = CAPACITY
    examples = devices * tok_rows // EX_LEN
    position = lax.axis_index("expert")
    levels = STRIPES.bit_length() - 1
    projected = jnp.dot(out_grad, out_proj, preferred_element_type=jnp.float32)
    matches = expert_ids[:, :, None] == jnp.arange(flight, dtype=jnp.int32)[None, None, :]
    weights = jnp.sum(jnp.where(matches, gate_weights[:, :, None], 0.0), axis=1)
    routed = jnp.any(matches, axis=1).T
    ranks = jnp.cumsum(routed.astype(jnp.int32), axis=1) - 1
    slot_ids = jnp.arange(capacity, dtype=jnp.int32)[None, :, None]
    select = (routed[:, None, :] & (ranks[:, None, :] == slot_ids)).astype(jnp.bfloat16)
    weighted = (weights[:, :, None] * projected[:, None, :]).astype(jnp.bfloat16)
    send_rows = jnp.einsum(
        "ect,td->ecd", select, tokens, preferred_element_type=jnp.float32
    ).astype(jnp.bfloat16)
    send_grads = jnp.einsum(
        "ect,ter->ecr", select, weighted, preferred_element_type=jnp.float32
    ).astype(jnp.bfloat16)
    rows_out = jnp.broadcast_to(send_rows[:, None], (flight, STRIPES, capacity, width)).reshape(
        devices, capacity, width
    )
    grads_out = jnp.broadcast_to(
        send_grads[:, None], (flight, STRIPES, capacity, rank_width)
    ).reshape(devices, capacity, rank_width)
    rows_in, grads_in = (
        lax.all_to_all(rows_out, "expert", split_axis=0, concat_axis=0, tiled=True),
        lax.all_to_all(grads_out, "expert", split_axis=0, concat_axis=0, tiled=True),
    )
    rows_in = rows_in[None]
    grads_in = grads_in[None]
    lead = rows_in.shape[0]
    per_source = rows_in.shape[2]
    flat_rows = rows_in.reshape(lead * devices * per_source, width)
    gate = jnp.dot(flat_rows, w_gate[0], preferred_element_type=jnp.float32)
    up = jnp.dot(flat_rows, w_up[0], preferred_element_type=jnp.float32)
    hidden = (jax.nn.silu(gate) * up).astype(jnp.bfloat16)
    inputs = jnp.dot(hidden, in_proj[0], preferred_element_type=jnp.float32)
    inputs = inputs.reshape(lead, examples, -1, rank_width)
    grads = grads_in.astype(jnp.float32).reshape(lead, examples, -1, rank_width)
    partial_value = jnp.einsum("abmi,abmj->ibj", grads, inputs, precision=lax.Precision.HIGHEST)
    partial_value = partial_value.reshape(rank_width, examples * rank_width)
    block = partial_value
    for bit in range(levels):
        block = block + partner(block, "expert", bit)
    rows_each = rank_width // STRIPES
    result = lax.dynamic_slice_in_dim(block, position % STRIPES * rows_each, rows_each, 0)
    return result


def solution(mesh):
    placed = (
        P(("groups", "expert"), None),
        P(("groups", "expert"), None),
        P(("groups", "expert"), None),
        P(("groups", "expert"), None),
        P("expert", None, None),
        P("expert", None, None),
        P("expert", None, None),
        P(),
    )
    return jax.shard_map(
        on_device,
        mesh=mesh,
        in_specs=placed,
        out_specs=P(("groups", "expert"), None),
        check_vma=False,
    )
```

profile of v0, /device:TPU:0, one launch (start us, length us, event | category | flops | bytes accessed | tf_op | source)
XLA Modules:
  0.0 83.2 jit_solution(16696163524351704674)
XLA Ops:
  0.0 0.0 copy-start
  0.0 0.8 %fusion.21 = pred[128,2]{0,1:T(4,128)(4,1)S(1)} fusion(s32[128,8]{0,1:T(8,128)} %param.10), kind=kLoop, calls=%fused_computation.20 | loop fusion | flops 3840 | bytes 4352 | tf_op jit(solution)/shard_map/reduce_or | solution.py:28
  0.8 0.3 reduce_window_sum.11
  1.2 0.7 select_reduce_fusion
  1.9 2.5 %fusion.29 = f32[128,64]{0,1:T(8,128)S(1)} fusion(bf16[128,7168]{1,0:T(8,128)(2,1)} %param.9, bf16[7168,64]{0,1:T(8,128)(2,1)} %param.15), kind=kOutput, calls=%fused_computation.28 | convolution fusion | flops 117440512 | bytes 2785280 | tf_op jit(solution)/shard_map/dot_general | solution.py:25
  4.4 0.1 convolution_convert_fusion.1
  4.5 0.7 reshape.45
  5.2 7.4 %all-to-all-start.1 = ((bf16[16,2,256]{2,1,0:T(2,128)(2,1)}), bf16[16,2,256]{2,1,0:T(2,128)(2,1)S(1)}, u32[]{:S(2)}, u32[]{:S(2)}) async-start(bf16[16,2,256]{2,1,0:T(2,128)(2,1)} %reshape.45), calls=%async_computation.1 | async-start | bytes 32768 | tf_op jit(solution)/shard_map/all_to_all | solution.py:47
  12.6 0.0 copy-done
  12.6 0.3 convolution_convert_fusion
  13.0 6.1 %all-to-all-done.1 = bf16[16,2,256]{2,1,0:T(2,128)(2,1)S(1)} async-done(((bf16[16,2,256]{2,1,0:T(2,128)(2,1)}), bf16[16,2,256]{2,1,0:T(2,128)(2,1)S(1)}, u32[]{:S(2)}, u32[]{:S(2)}) %all-to-all-start.1) | async-done | bytes 16416 | tf_op jit(solution)/shard_map/all_to_all | solution.py:47
  19.1 1.4 %broadcast_in_dim.16 = bf16[2,8,8,7168]{3,2,1,0:T(8,128)(2,1)} broadcast(bf16[2,8,7168]{2,1,0:T(8,128)(2,1)S(1)} %convolution_convert_fusion), dimensions={0,2,3} | broadcast | bytes 2064384 | tf_op jit(solution)/shard_map/broadcast_in_dim | solution.py:39
  20.5 4.4 %all-to-all-start = ((bf16[16,8,7168]{2,1,0:T(8,128)(2,1)}), bf16[16,8,7168]{2,1,0:T(8,128)(2,1)}, u32[]{:S(2)}, u32[]{:S(2)}) async-start(bf16[16,8,7168]{2,1,0:T(8,128)(2,1)} %bitcast.40), calls=%async_computation | async-start | bytes 3670016 | tf_op jit(solution)/shard_map/all_to_all | solution.py:46
  24.9 0.1 reshape.46
  25.0 36.4 %all-to-all-done = bf16[16,8,7168]{2,1,0:T(8,128)(2,1)} async-done(((bf16[16,8,7168]{2,1,0:T(8,128)(2,1)}), bf16[16,8,7168]{2,1,0:T(8,128)(2,1)}, u32[]{:S(2)}, u32[]{:S(2)}) %all-to-all-start) | async-done | bytes 1835040 | tf_op jit(solution)/shard_map/all_to_all | solution.py:46
  61.4 0.0 copy-start.1
  61.4 3.4 %fusion.2 = f32[128,256]{1,0:T(8,128)S(1)} fusion(bf16[1,7168,256]{2,1,0:T(8,128)(2,1)} %param.12, bf16[16,8,7168]{2,1,0:T(8,128)(2,1)} %all-to-all-done), kind=kOutput, calls=%fused_computation.3 | convolution fusion | flops 469762048 | bytes 5636096 | tf_op jit(solution)/shard_map/dot_general | solution.py:54
  64.8 0.3 copy-done.1
  65.1 0.0 copy-start.2
  65.1 2.2 %fusion.12 = bf16[128,256]{1,0:T(8,128)(2,1)S(1)} fusion(bf16[1,7168,256]{2,1,0:T(8,128)(2,1)S(1)} %copy-done.1, bf16[16,8,7168]{2,1,0:T(8,128)(2,1)} %all-to-all-done, f32[128,256]{1,0:T(8,128)S(1)} %fusion.2), kind=kOutput, calls=%fused_computation.9 | convolution fusion | flops 469958656 | bytes 5701632 | tf_op jit(solution)/shard_map/dot_general | solution.py:55
  67.3 0.0 copy-done.2
  67.3 0.1 fusion.17
  67.4 0.3 fusion.30
  67.8 0.1 copy.14
  67.9 0.8 %collective-permute-start = (f32[64,256]{1,0:T(8,128)S(1)}, f32[64,256]{1,0:T(8,128)S(1)}, u32[]{:S(2)}, u32[]{:S(2)}) collective-permute-start(f32[64,256]{1,0:T(8,128)S(1)} %copy.14), channel_id=1, source_target_pairs={{0,1},{1,0},{2,3},{3,2},{4,5},{5,4},{6,7},{7,6},{8,9},{9,8},{10,11... | collective-permute-start | bytes 196616 | tf_op jit(solution)/shard_map/ppermute | solution.py:12
  68.7 0.9 %collective-permute-done = f32[64,256]{1,0:T(8,128)S(1)} collective-permute-done((f32[64,256]{1,0:T(8,128)S(1)}, f32[64,256]{1,0:T(8,128)S(1)}, u32[]{:S(2)}, u32[]{:S(2)}) %collective-permute-start) | collective-permute-done | bytes 65568 | tf_op jit(solution)/shard_map/ppermute | solution.py:12
  69.6 3.1 %collective-permute-start.1 = (f32[64,256]{1,0:T(8,128)S(1)}, f32[64,256]{1,0:T(8,128)S(1)}, u32[]{:S(2)}, u32[]{:S(2)}) collective-permute-start(f32[64,256]{1,0:T(8,128)S(1)} %add.26), channel_id=1, source_target_pairs={{0,2},{1,3},{2,0},{3,1},{4,6},{5,7},{6,4},{7,5},{8,10},{9,11},{10,... | collective-permute-start | bytes 196616 | tf_op jit(solution)/shard_map/ppermute | solution.py:12
  72.7 2.6 %collective-permute-done.1 = f32[64,256]{1,0:T(8,128)S(1)} collective-permute-done((f32[64,256]{1,0:T(8,128)S(1)}, f32[64,256]{1,0:T(8,128)S(1)}, u32[]{:S(2)}, u32[]{:S(2)}) %collective-permute-start.1) | collective-permute-done | bytes 65568 | tf_op jit(solution)/shard_map/ppermute | solution.py:12
  75.3 5.1 %collective-permute-start.2 = (f32[64,256]{1,0:T(8,128)S(1)}, f32[64,256]{1,0:T(8,128)S(1)}, u32[]{:S(2)}, u32[]{:S(2)}) collective-permute-start(f32[64,256]{1,0:T(8,128)S(1)} %add.27), channel_id=1, source_target_pairs={{0,4},{1,5},{2,6},{3,7},{4,0},{5,1},{6,2},{7,3},{8,12},{9,13},{10,... | collective-permute-start | bytes 196616 | tf_op jit(solution)/shard_map/ppermute | solution.py:12
  80.4 2.2 %collective-permute-done.2 = f32[64,256]{1,0:T(8,128)S(1)} collective-permute-done((f32[64,256]{1,0:T(8,128)S(1)}, f32[64,256]{1,0:T(8,128)S(1)}, u32[]{:S(2)}, u32[]{:S(2)}) %collective-permute-start.2) | collective-permute-done | bytes 65568 | tf_op jit(solution)/shard_map/ppermute | solution.py:12
  82.6 0.6 dynamic-slice_add_fusion
  (5 shorter events, 0.0 us)
Async XLA Ops:
  0.0 12.6 %copy-start = (bf16[128,7168]{1,0:T(8,128)(2,1)S(1)}, bf16[128,7168]{1,0:T(8,128)(2,1)}, u32[]{:S(2)}) copy-start(bf16[128,7168]{1,0:T(8,128)(2,1)} %param.8) | copy-start | bytes 5505028
  5.2 13.9 %all-to-all-start.1 = ((bf16[16,2,256]{2,1,0:T(2,128)(2,1)}), bf16[16,2,256]{2,1,0:T(2,128)(2,1)S(1)}, u32[]{:S(2)}, u32[]{:S(2)}) async-start(bf16[16,2,256]{2,1,0:T(2,128)(2,1)} %reshape.45), calls=%async_computation.1 | async-start | bytes 32768 | tf_op jit(solution)/shard_map/all_to_all | solution.py:47
  20.5 40.9 %all-to-all-start = ((bf16[16,8,7168]{2,1,0:T(8,128)(2,1)}), bf16[16,8,7168]{2,1,0:T(8,128)(2,1)}, u32[]{:S(2)}, u32[]{:S(2)}) async-start(bf16[16,8,7168]{2,1,0:T(8,128)(2,1)} %bitcast.40), calls=%async_computation | async-start | bytes 3670016 | tf_op jit(solution)/shard_map/all_to_all | solution.py:46
  61.4 3.7 %copy-start.1 = (bf16[1,7168,256]{2,1,0:T(8,128)(2,1)S(1)}, bf16[1,7168,256]{2,1,0:T(8,128)(2,1)}, u32[]{:S(2)}) copy-start(bf16[1,7168,256]{2,1,0:T(8,128)(2,1)} %param.13) | copy-start | bytes 11010052
  65.1 2.2 %copy-start.2 = (bf16[1,256,64]{1,2,0:T(8,128)(2,1)S(1)}, bf16[1,256,64]{1,2,0:T(8,128)(2,1)}, u32[]{:S(2)}) copy-start(bf16[1,256,64]{1,2,0:T(8,128)(2,1)} %param.14) | copy-start | bytes 98308
  67.9 1.7 %collective-permute-start = (f32[64,256]{1,0:T(8,128)S(1)}, f32[64,256]{1,0:T(8,128)S(1)}, u32[]{:S(2)}, u32[]{:S(2)}) collective-permute-start(f32[64,256]{1,0:T(8,128)S(1)} %copy.14), channel_id=1, source_target_pairs={{0,1},{1,0},{2,3},{3,2},{4,5},{5,4},{6,7},{7,6},{8,9},{9,8},{10,11... | collective-permute-start | bytes 196616 | tf_op jit(solution)/shard_map/ppermute | solution.py:12
  69.6 5.7 %collective-permute-start.1 = (f32[64,256]{1,0:T(8,128)S(1)}, f32[64,256]{1,0:T(8,128)S(1)}, u32[]{:S(2)}, u32[]{:S(2)}) collective-permute-start(f32[64,256]{1,0:T(8,128)S(1)} %add.26), channel_id=1, source_target_pairs={{0,2},{1,3},{2,0},{3,1},{4,6},{5,7},{6,4},{7,5},{8,10},{9,11},{10,... | collective-permute-start | bytes 196616 | tf_op jit(solution)/shard_map/ppermute | solution.py:12
  75.3 7.3 %collective-permute-start.2 = (f32[64,256]{1,0:T(8,128)S(1)}, f32[64,256]{1,0:T(8,128)S(1)}, u32[]{:S(2)}, u32[]{:S(2)}) collective-permute-start(f32[64,256]{1,0:T(8,128)S(1)} %add.27), channel_id=1, source_target_pairs={{0,4},{1,5},{2,6},{3,7},{4,0},{5,1},{6,2},{7,3},{8,12},{9,13},{10,... | collective-permute-start | bytes 196616 | tf_op jit(solution)/shard_map/ppermute | solution.py:12
where the time goes:
time: 83.6 us; the launch traced here: 83.2 us
  waiting for transfers between devices  48.3 us (58%)
  starting transfers between devices  20.8 us (25%)
  matrix products  8.97 us (11%)
  local copies, waits for them, and re-layouts  2.57 us (3%)
  other arithmetic  2.5 us (3%)
    all_to_all x1, waiting for transfers between devices, on_device(): lax.all_to_all(rows_out, 'expert', split_axis=0, concat_axis=0, tiled=True)  36.4 us
    ppermute x3, starting transfers between devices, partner(): lax.ppermute(shard, axis, [(i, i ^ 1 << bit) for i in range(lax.axis_size...  8.99 us
    all_to_all x1, starting transfers between devices, on_device(): lax.all_to_all(grads_out, 'expert', split_axis=0, concat_axis=0, tiled=True)  7.39 us
    all_to_all x1, waiting for transfers between devices, on_device(): lax.all_to_all(grads_out, 'expert', split_axis=0, concat_axis=0, tiled=True)  6.14 us
    ppermute x3, waiting for transfers between devices, partner(): lax.ppermute(shard, axis, [(i, i ^ 1 << bit) for i in range(lax.axis_size...  5.76 us
    all_to_all x1, starting transfers between devices, on_device(): lax.all_to_all(rows_out, 'expert', split_axis=0, concat_axis=0, tiled=True)  4.41 us
    dot_general x1, matrix products, on_device(): gate = jnp.dot(flat_rows, w_gate[0], preferred_element_type=jnp.float32)  3.39 us
    dot_general x1, matrix products, on_device(): projected = jnp.dot(out_grad, out_proj, preferred_element_type=jnp.float32)  2.48 us
  transfers between devices with their start and end apart: 5, of which 5 were waited for; matrix products, arithmetic and copies ran while one was open for 1% of the time, Pallas kernels for 0%

commit v1 on v0

v1 whole, which is shorter than its diff:
```python
import functools
import jax
import jax.numpy as jnp
from jax import lax
from jax.experimental import pallas as pl
from jax.experimental.pallas import tpu as pltpu
from jax.sharding import PartitionSpec as P

STRIPES = 8
EX_LEN = 512
CAPACITY = 8
HALVES = 2
GROUP = 16
BF16 = jnp.bfloat16
F32 = jnp.float32


def toggled(m, bit):
    size = 1 << bit
    return m + size - 2 * size * lax.rem(lax.div(m, size), 2)


def kernel(
    n,
    tokens,
    out_grad,
    ids_hbm,
    gates_hbm,
    w_gate,
    w_up,
    in_proj,
    out_proj,
    out,
    tok,
    og,
    ids,
    gw,
    wg,
    wu,
    ip,
    op,
    outgoing,
    rows,
    grads_out,
    grads_in,
    sums_out,
    sums_in,
    load_sem,
    local_sem,
    send_sem,
    recv_sem,
    gsend_sem,
    grecv_sem,
    ssend_sem,
    srecv_sem,
):
    flight = n // STRIPES
    me = lax.axis_index("expert")
    octet, member = lax.div(me, STRIPES), lax.rem(me, STRIPES)
    base = octet * STRIPES
    width = tok.shape[1]
    tok_rows = tok.shape[0]
    rank = op.shape[1]
    part = rows.shape[3]

    loads = [
        pltpu.make_async_copy(src, dst, load_sem.at[i])
        for i, (src, dst) in enumerate(
            (
                (ids_hbm, ids),
                (gates_hbm, gw),
                (tokens, tok),
                (out_grad, og),
                (out_proj, op),
                (in_proj.at[0], ip),
                (w_gate.at[0], wg),
                (w_up.at[0], wu),
            )
        )
    ]
    for load in loads:
        load.start()

    barrier = pltpu.get_barrier_semaphore()

    def greet(step, carry):
        pl.semaphore_signal(barrier, inc=1, device_id={"expert": lax.rem(me + step, n)})
        return carry

    lax.fori_loop(1, n, greet, 0)

    loads[0].wait()
    loads[1].wait()
    lanes = max(128, flight * CAPACITY)
    lane = lax.broadcasted_iota(jnp.int32, (tok_rows, lanes), 1)
    expert_of, slot_of = lax.div(lane, CAPACITY), lax.rem(lane, CAPACITY)
    routed = jnp.zeros((tok_rows, lanes), F32)
    weight = jnp.zeros((tok_rows, lanes), F32)
    for k in range(ids.shape[1]):
        match = ids[:, k : k + 1] == expert_of
        routed = jnp.where(match, 1.0, routed)
        weight = weight + jnp.where(match, gw[:, k : k + 1], 0.0)
    below = lax.broadcasted_iota(jnp.int32, (tok_rows, tok_rows), 0) >= lax.broadcasted_iota(
        jnp.int32, (tok_rows, tok_rows), 1
    )
    ranks = jnp.dot(
        jnp.where(below, 1.0, 0.0).astype(BF16), routed.astype(BF16), preferred_element_type=F32
    )
    taken = (routed > 0.0) & (ranks == (slot_of + 1).astype(F32))
    used = flight * CAPACITY
    sel = jnp.where(taken, 1.0, 0.0).T[:used].astype(BF16)
    slot_weight = jnp.sum(jnp.where(taken, weight, 0.0).T[:used], axis=1, keepdims=True)

    loads[2].wait()
    half = width // 2
    for h in range(HALVES):
        lo = h * part
        left = jnp.dot(sel, tok[:, lo : lo + part], preferred_element_type=F32)
        right = jnp.dot(sel, tok[:, half + lo : half + lo + part], preferred_element_type=F32)
        for e in range(flight):
            at = slice(e * CAPACITY, (e + 1) * CAPACITY)
            outgoing[h, e] = jnp.concatenate([left[at], right[at]], axis=0).astype(BF16)

    pl.semaphore_wait(barrier, n - 1)

    def send(src, source, h, target):
        pltpu.make_async_remote_copy(
            src_ref=src,
            dst_ref=rows.at[h, source],
            send_sem=send_sem,
            recv_sem=recv_sem.at[h, source],
            device_id={"expert": target},
        ).start()

    def arrived(source, h):
        pltpu.make_async_copy(
            rows.at[h, source], rows.at[h, source], recv_sem.at[h, source]
        ).wait()

    core, near, far = (base + toggled(member, bit) for bit in range(3))

    def across(step, carry):
        e = lax.rem(octet + step, flight)
        for h in range(HALVES):
            send(outgoing.at[h, e], me, h, e * STRIPES + member)
        return carry

    lax.fori_loop(1, flight, across, 0)
    own = []
    for h in range(HALVES):
        for target in (far, near, core):
            send(outgoing.at[h, octet], me, h, target)
        keep = pltpu.make_async_copy(outgoing.at[h, octet], rows.at[h, me], local_sem.at[h])
        keep.start()
        own.append(keep)

    loads[3].wait()
    loads[4].wait()
    chosen = jnp.dot(sel, og[...], preferred_element_type=F32).astype(BF16)
    projected = jnp.dot(chosen, op[...], preferred_element_type=F32)
    weighted = (slot_weight * projected).astype(BF16).astype(F32)
    weighted = jnp.concatenate([weighted, jnp.zeros_like(weighted)], axis=1)
    for e in range(flight):
        grads_out[e] = weighted[e * CAPACITY : (e + 1) * CAPACITY]

    def send_grads(step, carry):
        target = lax.rem(me + step, n)
        pltpu.make_async_remote_copy(
            src_ref=grads_out.at[lax.div(target, STRIPES)],
            dst_ref=grads_in.at[me],
            send_sem=gsend_sem,
            recv_sem=grecv_sem,
            device_id={"expert": target},
        ).start()
        return carry

    lax.fori_loop(1, n, send_grads, 0)
    grads_in[me] = grads_out[octet]

    def spread(at):
        near_source, far_source = at + toggled(member, 1), at + toggled(member, 2)
        arrived(far_source, 1)
        send(rows.at[1, far_source], far_source, 1, near)
        send(rows.at[1, far_source], far_source, 1, core)
        arrived(near_source, 0)
        send(rows.at[0, near_source], near_source, 0, far)
        send(rows.at[0, near_source], near_source, 0, core)
        arrived(near_source, 1)
        send(rows.at[1, near_source], near_source, 1, core)
        arrived(far_source, 0)
        send(rows.at[0, far_source], far_source, 0, core)

    def finish(at):
        diagonal = at + toggled(toggled(member, 1), 2)
        for h in range(HALVES):
            arrived(diagonal, h)
            send(rows.at[h, diagonal], diagonal, h, core)

    def settle(at):
        for bits in ((), (1,), (2,), (1, 2)):
            source = toggled(member, 0)
            for bit in bits:
                source = toggled(source, bit)
            for h in range(HALVES):
                arrived(at + source, h)

    spread(base)

    def onward(step, carry):
        at = lax.rem(octet + step, flight) * STRIPES
        for h in (1, 0):
            arrived(at + member, h)
            for target in (far, near, core):
                send(rows.at[h, at + member], at + member, h, target)
        return carry

    lax.fori_loop(1, flight, onward, 0)
    finish(base)

    def rest(step, carry):
        at = lax.rem(octet + step, flight) * STRIPES
        spread(at)
        finish(at)
        return carry

    lax.fori_loop(1, flight, rest, 0)

    loads[5].wait()
    examples_each = GROUP * tok_rows // EX_LEN
    cols = examples_each * rank
    repeat = jnp.where(
        lax.rem(lax.broadcasted_iota(jnp.int32, (rank, cols), 1), rank)
        == lax.broadcasted_iota(jnp.int32, (rank, cols), 0),
        1.0,
        0.0,
    ).astype(BF16)
    ip_wide = jnp.dot(ip[...], repeat, preferred_element_type=F32).astype(BF16)
    loads[6].wait()
    loads[7].wait()

    def settled(step, carry):
        settle(step * STRIPES)
        return carry

    lax.fori_loop(0, flight, settled, 0)
    for keep in own:
        keep.wait()
    pltpu.make_async_copy(
        grads_in.at[pl.ds(0, n - 1)], grads_in.at[pl.ds(0, n - 1)], grecv_sem
    ).wait()

    count = GROUP * CAPACITY
    keep_cols = lax.div(
        lax.broadcasted_iota(jnp.int32, (count, cols), 0), EX_LEN // tok_rows * CAPACITY
    ) == lax.div(lax.broadcasted_iota(jnp.int32, (count, cols), 1), rank)

    def block(g, carry):
        sources = pl.ds(pl.multiple_of(g * GROUP, GROUP), GROUP)
        gate = jnp.zeros((count, wg.shape[1]), F32)
        up = jnp.zeros((count, wg.shape[1]), F32)
        for h in range(HALVES):
            both = rows[h, sources].astype(F32)
            for side in range(2):
                x = both[:, side * CAPACITY : (side + 1) * CAPACITY].reshape(count, part)
                x = x.astype(BF16)
                lo = side * half + h * part
                gate = gate + jnp.dot(x, wg[lo : lo + part], preferred_element_type=F32)
                up = up + jnp.dot(x, wu[lo : lo + part], preferred_element_type=F32)
        hidden = (gate / (1.0 + jnp.exp(-gate)) * up).astype(BF16)
        inputs = jnp.dot(hidden, ip_wide, preferred_element_type=F32)
        inputs = jnp.where(keep_cols, inputs, 0.0)
        high = inputs.astype(BF16)
        rest_of = inputs - high.astype(F32)
        mid = rest_of.astype(BF16)
        low = (rest_of - mid.astype(F32)).astype(BF16)
        g_rows = grads_in[sources].reshape(count, grads_in.shape[2]).astype(BF16)
        contract = (((0,), (0,)), ((), ()))
        total = lax.dot_general(
            jnp.concatenate([g_rows, g_rows, g_rows], axis=0),
            jnp.concatenate([low, mid, high], axis=0),
            contract,
            preferred_element_type=F32,
        )
        sums_out[:, :, pl.ds(pl.multiple_of(g * cols, cols), cols)] = total[:rank].reshape(
            STRIPES, rank // STRIPES, cols
        )
        return carry

    lax.fori_loop(0, n // GROUP, block, 0)

    for step in range(1, STRIPES):
        target = lax.rem(member + step, STRIPES)
        pltpu.make_async_remote_copy(
            src_ref=sums_out.at[target],
            dst_ref=sums_in.at[member],
            send_sem=ssend_sem,
            recv_sem=srecv_sem,
            device_id={"expert": base + target},
        ).start()
    sums_in[member] = sums_out[member]
    others = pl.ds(0, STRIPES - 1)
    pltpu.make_async_copy(
        rows.at[:, pl.ds(0, n - 1)], rows.at[:, pl.ds(0, n - 1)], send_sem
    ).wait()
    pltpu.make_async_copy(
        grads_in.at[pl.ds(0, n - 1)], grads_in.at[pl.ds(0, n - 1)], gsend_sem
    ).wait()
    pltpu.make_async_copy(sums_in.at[others], sums_in.at[others], srecv_sem).wait()
    total = sums_in[0]
    for j in range(1, STRIPES):
        total = total + sums_in[j]
    out[...] = total
    pltpu.make_async_copy(sums_in.at[others], sums_in.at[others], ssend_sem).wait()


def on_device(tokens, out_grad, expert_ids, gate_weights, w_gate, w_up, in_proj, out_proj):
    n = lax.axis_size("expert")
    flight = n // STRIPES
    tok_rows, width = tokens.shape
    hidden_units = w_gate.shape[2]
    rank = out_proj.shape[1]
    part = width // 2 // HALVES
    out_cols = n * tok_rows // EX_LEN * rank
    rank_each = rank // STRIPES
    dma = pltpu.SemaphoreType.DMA
    return pl.pallas_call(
        functools.partial(kernel, n),
        out_shape=jax.ShapeDtypeStruct((rank_each, out_cols), F32),
        in_specs=[pl.BlockSpec(memory_space=pl.ANY)] * 8,
        out_specs=pl.BlockSpec(memory_space=pltpu.VMEM),
        scratch_shapes=[
            pltpu.VMEM((tok_rows, width), BF16),
            pltpu.VMEM((tok_rows, width), BF16),
            pltpu.VMEM(expert_ids.shape, jnp.int32),
            pltpu.VMEM(gate_weights.shape, F32),
            pltpu.VMEM((width, hidden_units), BF16),
            pltpu.VMEM((width, hidden_units), BF16),
            pltpu.VMEM((hidden_units, rank), BF16),
            pltpu.VMEM((width, rank), BF16),
            pltpu.VMEM((HALVES, flight, 2 * CAPACITY, part), BF16),
            pltpu.VMEM((HALVES, n, 2 * CAPACITY, part), BF16),
            pltpu.VMEM((flight, CAPACITY, 2 * rank), F32),
            pltpu.VMEM((n, CAPACITY, 2 * rank), F32),
            pltpu.VMEM((STRIPES, rank_each, out_cols), F32),
            pltpu.VMEM((STRIPES, rank_each, out_cols), F32),
            dma((8,)),
            dma((HALVES,)),
            dma,
            dma((HALVES, n)),
            dma,
            dma,
            dma,
            dma,
        ],
        compiler_params=pltpu.CompilerParams(
            collective_id=0, has_side_effects=True, vmem_limit_bytes=56 * 1024 * 1024
        ),
    )(tokens, out_grad, expert_ids, gate_weights, w_gate, w_up, in_proj, out_proj)


def solution(mesh):
    placed = (
        P(("groups", "expert"), None),
        P(("groups", "expert"), None),
        P(("groups", "expert"), None),
        P(("groups", "expert"), None),
        P("expert", None, None),
        P("expert", None, None),
        P("expert", None, None),
        P(),
    )
    return jax.shard_map(
        on_device,
        mesh=mesh,
        in_specs=placed,
        out_specs=P(("groups", "expert"), None),
        check_vma=False,
    )
```

time: 83.6 us -> 36 us (0.43)
  waiting for transfers between devices: 48.3 us -> 0 us
  Pallas kernels: 0 us -> 27.5 us
  starting transfers between devices: 20.8 us -> 0 us
  matrix products: 8.97 us -> 0 us
  local copies, waits for them, and re-layouts: 2.57 us -> 8.21 us
  other arithmetic: 2.5 us -> 0 us
    all_to_all x2 -> x0, waiting for transfers between devices: 42.6 us -> none  [the longest x1 36.4 us: on_device(): lax.all_to_all(rows_out, 'expert', split_axis=0, concat_axis=0, tiled=True)]
    pallas_call x0 -> x1, Pallas kernels: none -> 27.5 us  [on_device(): pl.pallas_call(functools.partial(kernel, n), out_shape=jax.ShapeDtypeStru...]
    all_to_all x2 -> x0, starting transfers between devices: 11.8 us -> none  [the longest x1 7.39 us: on_device(): lax.all_to_all(grads_out, 'expert', split_axis=0, concat_axis=0, tiled=True)]
    ppermute x3 -> x0, starting transfers between devices: 8.99 us -> none  [partner(): lax.ppermute(shard, axis, [(i, i ^ 1 << bit) for i in range(lax.axis_size...]
    dot_general x7 -> x0, matrix products: 8.97 us -> none  [the longest x1 3.39 us: on_device(): gate = jnp.dot(flat_rows, w_gate[0], preferred_element_type=jnp.float32)]
    unnamed x8 -> x5, local copies, waits for them, and re-layouts: 1.09 us -> 8.21 us
    ppermute x3 -> x0, waiting for transfers between devices: 5.76 us -> none  [partner(): lax.ppermute(shard, axis, [(i, i ^ 1 << bit) for i in range(lax.axis_size...]
    broadcast_in_dim x2 -> x0, local copies, waits for them, and re-layouts: 1.4 us -> none  [the longest x1 1.4 us: on_device(): jnp.broadcast_to(send_rows[:, None], (flight, STRIPES, capacity, width))]
  transfers between devices with their start and end apart: 5 -> 0, of which waited for: 5 -> 0; matrix products, arithmetic and copies ran while one was open for 1% -> 0% of each run, Pallas kernels for 0% -> 0%
where the time goes in v1:
time: 36 us; the launch traced here: 35.7 us
  Pallas kernels  27.5 us (76%)
  local copies, waits for them, and re-layouts  8.21 us (23%)
    pallas_call x1, Pallas kernels, on_device(): pl.pallas_call(functools.partial(kernel, n), out_shape=jax.ShapeDtypeStru...  27.5 us
    unnamed x5, local copies, waits for them, and re-layouts  8.21 us

profile of v1, /device:TPU:0, one launch (start us, length us, event | category | flops | bytes accessed | tf_op | source)
XLA Modules:
  0.0 35.7 jit_solution(3794751132305420020)
XLA Ops:
  0.0 1.4 %copy.9.ids_hbm = s32[128,8]{1,0:T(8,128)} copy(s32[128,8]{0,1:T(8,128)} %param.10) | data formatting | bytes 8192 | tf_op args[2]
  1.4 1.4 %copy.10.gates_hbm = f32[128,8]{1,0:T(8,128)} copy(f32[128,8]{0,1:T(8,128)} %param.11) | data formatting | bytes 8192 | tf_op args[3]
  2.8 1.5 %copy.11.in_proj = bf16[1,256,64]{2,1,0:T(8,128)(2,1)} copy(bf16[1,256,64]{1,2,0:T(8,128)(2,1)} %param.14) | data formatting | bytes 65536 | tf_op args[6]
  4.3 2.6 %copy.12.out_proj = bf16[7168,64]{1,0:T(8,128)(2,1)} copy(bf16[7168,64]{0,1:T(8,128)(2,1)} %param.15) | data formatting | bytes 1835008 | tf_op args[7]
  6.9 27.5 %shard_map.82 = f32[8,256]{1,0:T(8,128)} custom-call(bf16[128,7168]{1,0:T(8,128)(2,1)} %tokens.1, bf16[128,7168]{1,0:T(8,128)(2,1)} %out_grad.1, s32[128,8]{1,0:T(8,128)} %copy.9.ids_hbm, f32[128,8]{1,0:T(8,128)} %copy.10.gates_hbm, bf16[1,7168,256]{2,1,0:T(8,128)(2,1)} %w_gate.1, bf16[1,7168,256]{2,1,0:T(8,128)(2,1)} %w_up.1, ...), custom_call_target="tpu_custom_call" | custom-call | tf_op jit(solution)/shard_map/pallas_call | solution.py:326
  34.4 1.3 %copy.14 = f32[8,256]{1,0:T(8,128)} copy(f32[8,256]{1,0:T(8,128)} %shard_map.82) | data formatting | bytes 16384

commit v2 on v1

--- a/solution.py
+++ b/solution.py
@@ -13,6 +13,7 @@
 GROUP = 16
 BF16 = jnp.bfloat16
 F32 = jnp.float32
+BY_LAST = (((1,), (1,)), ((), ()))
 
 
 def toggled(m, bit):
@@ -60,7 +61,7 @@
     base = octet * STRIPES
     width = tok.shape[1]
     tok_rows = tok.shape[0]
-    rank = op.shape[1]
+    rank = op.shape[0]
     part = rows.shape[3]
 
     loads = [
@@ -91,25 +92,24 @@
 
     loads[0].wait()
     loads[1].wait()
-    lanes = max(128, flight * CAPACITY)
-    lane = lax.broadcasted_iota(jnp.int32, (tok_rows, lanes), 1)
-    expert_of, slot_of = lax.div(lane, CAPACITY), lax.rem(lane, CAPACITY)
-    routed = jnp.zeros((tok_rows, lanes), F32)
-    weight = jnp.zeros((tok_rows, lanes), F32)
-    for k in range(ids.shape[1]):
-        match = ids[:, k : k + 1] == expert_of
+    used = flight * CAPACITY
+    line = lax.broadcasted_iota(jnp.int32, (used, tok_rows), 0)
+    expert_of, slot_of = lax.div(line, CAPACITY), lax.rem(line, CAPACITY)
+    routed = jnp.zeros((used, tok_rows), F32)
+    weight = jnp.zeros((used, tok_rows), F32)
+    for k in range(ids.shape[0]):
+        match = ids[k : k + 1] == expert_of
         routed = jnp.where(match, 1.0, routed)
-        weight = weight + jnp.where(match, gw[:, k : k + 1], 0.0)
-    below = lax.broadcasted_iota(jnp.int32, (tok_rows, tok_rows), 0) >= lax.broadcasted_iota(
+        weight = weight + jnp.where(match, gw[k : k + 1], 0.0)
+    upto = lax.broadcasted_iota(jnp.int32, (tok_rows, tok_rows), 0) <= lax.broadcasted_iota(
         jnp.int32, (tok_rows, tok_rows), 1
     )
     ranks = jnp.dot(
-        jnp.where(below, 1.0, 0.0).astype(BF16), routed.astype(BF16), preferred_element_type=F32
+        routed.astype(BF16), jnp.where(upto, 1.0, 0.0).astype(BF16), preferred_element_type=F32
     )
     taken = (routed > 0.0) & (ranks == (slot_of + 1).astype(F32))
-    used = flight * CAPACITY
-    sel = jnp.where(taken, 1.0, 0.0).T[:used].astype(BF16)
-    slot_weight = jnp.sum(jnp.where(taken, weight, 0.0).T[:used], axis=1, keepdims=True)
+    sel = jnp.where(taken, 1.0, 0.0).astype(BF16)
+    slot_weight = jnp.sum(jnp.where(taken, weight, 0.0), axis=1, keepdims=True)
 
     loads[2].wait()
     half = width // 2
@@ -157,7 +157,7 @@
     loads[3].wait()
     loads[4].wait()
     chosen = jnp.dot(sel, og[...], preferred_element_type=F32).astype(BF16)
-    projected = jnp.dot(chosen, op[...], preferred_element_type=F32)
+    projected = lax.dot_general(chosen, op[...], BY_LAST, preferred_element_type=F32)
     weighted = (slot_weight * projected).astype(BF16).astype(F32)
     weighted = jnp.concatenate([weighted, jnp.zeros_like(weighted)], axis=1)
     for e in range(flight):
@@ -228,13 +228,7 @@
     loads[5].wait()
     examples_each = GROUP * tok_rows // EX_LEN
     cols = examples_each * rank
-    repeat = jnp.where(
-        lax.rem(lax.broadcasted_iota(jnp.int32, (rank, cols), 1), rank)
-        == lax.broadcasted_iota(jnp.int32, (rank, cols), 0),
-        1.0,
-        0.0,
-    ).astype(BF16)
-    ip_wide = jnp.dot(ip[...], repeat, preferred_element_type=F32).astype(BF16)
+    ip_wide = jnp.concatenate([ip[...]] * examples_each, axis=0)
     loads[6].wait()
     loads[7].wait()
 
@@ -267,7 +261,7 @@
                 gate = gate + jnp.dot(x, wg[lo : lo + part], preferred_element_type=F32)
                 up = up + jnp.dot(x, wu[lo : lo + part], preferred_element_type=F32)
         hidden = (gate / (1.0 + jnp.exp(-gate)) * up).astype(BF16)
-        inputs = jnp.dot(hidden, ip_wide, preferred_element_type=F32)
+        inputs = lax.dot_general(hidden, ip_wide, BY_LAST, preferred_element_type=F32)
         inputs = jnp.where(keep_cols, inputs, 0.0)
         high = inputs.astype(BF16)
         rest_of = inputs - high.astype(F32)
@@ -331,12 +325,12 @@
         scratch_shapes=[
             pltpu.VMEM((tok_rows, width), BF16),
             pltpu.VMEM((tok_rows, width), BF16),
-            pltpu.VMEM(expert_ids.shape, jnp.int32),
-            pltpu.VMEM(gate_weights.shape, F32),
+            pltpu.VMEM(expert_ids.shape[::-1], jnp.int32),
+            pltpu.VMEM(gate_weights.shape[::-1], F32),
             pltpu.VMEM((width, hidden_units), BF16),
             pltpu.VMEM((width, hidden_units), BF16),
-            pltpu.VMEM((hidden_units, rank), BF16),
-            pltpu.VMEM((width, rank), BF16),
+            pltpu.VMEM((rank, hidden_units), BF16),
+            pltpu.VMEM((rank, width), BF16),
             pltpu.VMEM((HALVES, flight, 2 * CAPACITY, part), BF16),
             pltpu.VMEM((HALVES, n, 2 * CAPACITY, part), BF16),
             pltpu.VMEM((flight, CAPACITY, 2 * rank), F32),
@@ -355,7 +349,16 @@
         compiler_params=pltpu.CompilerParams(
             collective_id=0, has_side_effects=True, vmem_limit_bytes=56 * 1024 * 1024
         ),
-    )(tokens, out_grad, expert_ids, gate_weights, w_gate, w_up, in_proj, out_proj)
+    )(
+        tokens,
+        out_grad,
+        expert_ids.T,
+        gate_weights.T,
+        w_gate,
+        w_up,
+        in_proj.transpose(0, 2, 1),
+        out_proj.T,
+    )
 
 
 def solution(mesh):

time: 36 us -> 29.3 us (0.81)
  local copies, waits for them, and re-layouts: 8.21 us -> 1.3 us
    unnamed x5 -> x1, local copies, waits for them, and re-layouts: 8.21 us -> 1.3 us
where the time goes in v2:
time: 29.3 us; the launch traced here: 29 us
  Pallas kernels  27.7 us (95%)
  local copies, waits for them, and re-layouts  1.3 us (4%)
    pallas_call x1, Pallas kernels, on_device(): pl.pallas_call(functools.partial(kernel, n), out_shape=jax.ShapeDtypeStru...  27.7 us
    unnamed x1, local copies, waits for them, and re-layouts  1.3 us

profile of v2, /device:TPU:0, one launch (start us, length us, event | category | flops | bytes accessed | tf_op | source)
XLA Modules:
  0.0 29.0 jit_solution(8998691129925760234)
XLA Ops:
  0.0 27.7 %shard_map.82 = f32[8,256]{1,0:T(8,128)} custom-call(bf16[128,7168]{1,0:T(8,128)(2,1)} %tokens.1, bf16[128,7168]{1,0:T(8,128)(2,1)} %out_grad.1, s32[8,128]{1,0:T(8,128)} %bitcast.6, f32[8,128]{1,0:T(8,128)} %bitcast.7, bf16[1,7168,256]{2,1,0:T(8,128)(2,1)} %w_gate.1, bf16[1,7168,256]{2,1,0:T(8,128)(2,1)} %w_up.1, bf16[1,64,256]{2,1,0:T(8,128)(2,1)} %bitcast.5, ...), custom_call_target="tpu_custom_call" | custom-call | tf_op jit(solution)/shard_map/pallas_call | solution.py:320
  27.7 1.3 %copy.10 = f32[8,256]{1,0:T(8,128)} copy(f32[8,256]{1,0:T(8,128)} %shard_map.82) | data formatting | bytes 16384

commit v3 on v2

--- a/solution.py
+++ b/solution.py
@@ -9,8 +9,9 @@
 STRIPES = 8
 EX_LEN = 512
 CAPACITY = 8
-HALVES = 2
-GROUP = 16
+PIECES = 2
+ORDER = (1, 0)
+DIAGONAL_BY_FAR = (0,)
 BF16 = jnp.bfloat16
 F32 = jnp.float32
 BY_LAST = (((1,), (1,)), ((), ()))
@@ -84,11 +85,16 @@
 
     barrier = pltpu.get_barrier_semaphore()
 
-    def greet(step, carry):
-        pl.semaphore_signal(barrier, inc=1, device_id={"expert": lax.rem(me + step, n)})
-        return carry
-
-    lax.fori_loop(1, n, greet, 0)
+    def greet(target):
+        pl.semaphore_signal(barrier, inc=1, device_id={"expert": target})
+
+    def greet_across(step, carry):
+        greet(lax.rem(octet + step, flight) * STRIPES + member)
+        return carry
+
+    lax.fori_loop(1, flight, greet_across, 0)
+    for step in range(1, STRIPES):
+        greet(base + lax.rem(member + step, STRIPES))
 
     loads[0].wait()
     loads[1].wait()
@@ -113,7 +119,7 @@
 
     loads[2].wait()
     half = width // 2
-    for h in range(HALVES):
+    for h in range(PIECES):
         lo = h * part
         left = jnp.dot(sel, tok[:, lo : lo + part], preferred_element_type=F32)
         right = jnp.dot(sel, tok[:, half + lo : half + lo + part], preferred_element_type=F32)
@@ -121,7 +127,7 @@
             at = slice(e * CAPACITY, (e + 1) * CAPACITY)
             outgoing[h, e] = jnp.concatenate([left[at], right[at]], axis=0).astype(BF16)
 
-    pl.semaphore_wait(barrier, n - 1)
+    pl.semaphore_wait(barrier, flight - 1 + STRIPES - 1)
 
     def send(src, source, h, target):
         pltpu.make_async_remote_copy(
@@ -141,13 +147,13 @@
 
     def across(step, carry):
         e = lax.rem(octet + step, flight)
-        for h in range(HALVES):
+        for h in ORDER:
             send(outgoing.at[h, e], me, h, e * STRIPES + member)
         return carry
 
     lax.fori_loop(1, flight, across, 0)
     own = []
-    for h in range(HALVES):
+    for h in ORDER:
         for target in (far, near, core):
             send(outgoing.at[h, octet], me, h, target)
         keep = pltpu.make_async_copy(outgoing.at[h, octet], rows.at[h, me], local_sem.at[h])
@@ -164,35 +170,47 @@
         grads_out[e] = weighted[e * CAPACITY : (e + 1) * CAPACITY]
 
     def send_grads(step, carry):
-        target = lax.rem(me + step, n)
+        e = lax.rem(octet + step, flight)
         pltpu.make_async_remote_copy(
-            src_ref=grads_out.at[lax.div(target, STRIPES)],
-            dst_ref=grads_in.at[me],
-            send_sem=gsend_sem,
-            recv_sem=grecv_sem,
-            device_id={"expert": target},
+            src_ref=grads_out.at[e],
+            dst_ref=grads_in.at[member, octet],
+            send_sem=gsend_sem.at[0],
+            recv_sem=grecv_sem.at[0],
+            device_id={"expert": e * STRIPES + member},
         ).start()
         return carry
 
-    lax.fori_loop(1, n, send_grads, 0)
-    grads_in[me] = grads_out[octet]
+    lax.fori_loop(1, flight, send_grads, 0)
+    grads_in[member, octet] = grads_out[octet]
+
+    def spread_grads():
+        if flight > 1:
+            some = grads_in.at[0, pl.ds(0, flight - 1)]
+            pltpu.make_async_copy(some, some, grecv_sem.at[0]).wait()
+        for step in range(1, STRIPES):
+            pltpu.make_async_remote_copy(
+                src_ref=grads_in.at[member],
+                dst_ref=grads_in.at[member],
+                send_sem=gsend_sem.at[1],
+                recv_sem=grecv_sem.at[1],
+                device_id={"expert": base + lax.rem(member + step, STRIPES)},
+            ).start()
 
     def spread(at):
         near_source, far_source = at + toggled(member, 1), at + toggled(member, 2)
-        arrived(far_source, 1)
-        send(rows.at[1, far_source], far_source, 1, near)
-        send(rows.at[1, far_source], far_source, 1, core)
-        arrived(near_source, 0)
-        send(rows.at[0, near_source], near_source, 0, far)
-        send(rows.at[0, near_source], near_source, 0, core)
-        arrived(near_source, 1)
-        send(rows.at[1, near_source], near_source, 1, core)
-        arrived(far_source, 0)
-        send(rows.at[0, far_source], far_source, 0, core)
+        for h in ORDER:
+            arrived(far_source, h)
+            if h not in DIAGONAL_BY_FAR:
+                send(rows.at[h, far_source], far_source, h, near)
+            send(rows.at[h, far_source], far_source, h, core)
+            arrived(near_source, h)
+            if h in DIAGONAL_BY_FAR:
+                send(rows.at[h, near_source], near_source, h, far)
+            send(rows.at[h, near_source], near_source, h, core)
 
     def finish(at):
         diagonal = at + toggled(toggled(member, 1), 2)
-        for h in range(HALVES):
+        for h in ORDER:
             arrived(diagonal, h)
             send(rows.at[h, diagonal], diagonal, h, core)
 
@@ -201,58 +219,46 @@
             source = toggled(member, 0)
             for bit in bits:
                 source = toggled(source, bit)
-            for h in range(HALVES):
+            for h in range(PIECES):
                 arrived(at + source, h)
 
     spread(base)
 
     def onward(step, carry):
         at = lax.rem(octet + step, flight) * STRIPES
-        for h in (1, 0):
+        for h in ORDER:
             arrived(at + member, h)
             for target in (far, near, core):
                 send(rows.at[h, at + member], at + member, h, target)
         return carry
 
     lax.fori_loop(1, flight, onward, 0)
+    spread_grads()
     finish(base)
 
-    def rest(step, carry):
-        at = lax.rem(octet + step, flight) * STRIPES
-        spread(at)
-        finish(at)
-        return carry
-
-    lax.fori_loop(1, flight, rest, 0)
-
     loads[5].wait()
-    examples_each = GROUP * tok_rows // EX_LEN
+    examples_each = STRIPES * tok_rows // EX_LEN
     cols = examples_each * rank
     ip_wide = jnp.concatenate([ip[...]] * examples_each, axis=0)
     loads[6].wait()
     loads[7].wait()
 
-    def settled(step, carry):
-        settle(step * STRIPES)
-        return carry
-
-    lax.fori_loop(0, flight, settled, 0)
     for keep in own:
         keep.wait()
-    pltpu.make_async_copy(
-        grads_in.at[pl.ds(0, n - 1)], grads_in.at[pl.ds(0, n - 1)], grecv_sem
-    ).wait()
-
-    count = GROUP * CAPACITY
+    others = pl.ds(0, STRIPES - 1)
+    pltpu.make_async_copy(grads_in.at[others], grads_in.at[others], grecv_sem.at[1]).wait()
+
+    count = STRIPES * CAPACITY
     keep_cols = lax.div(
         lax.broadcasted_iota(jnp.int32, (count, cols), 0), EX_LEN // tok_rows * CAPACITY
     ) == lax.div(lax.broadcasted_iota(jnp.int32, (count, cols), 1), rank)
 
-    def block(g, carry):
-        sources = pl.ds(pl.multiple_of(g * GROUP, GROUP), GROUP)
+    def block(g):
+        settle(g * STRIPES)
+        sources = pl.ds(pl.multiple_of(g * STRIPES, STRIPES), STRIPES)
         gate = jnp.zeros((count, wg.shape[1]), F32)
         up = jnp.zeros((count, wg.shape[1]), F32)
-        for h in range(HALVES):
+        for h in range(PIECES):
             both = rows[h, sources].astype(F32)
             for side in range(2):
                 x = both[:, side * CAPACITY : (side + 1) * CAPACITY].reshape(count, part)
@@ -267,7 +273,7 @@
         rest_of = inputs - high.astype(F32)
         mid = rest_of.astype(BF16)
         low = (rest_of - mid.astype(F32)).astype(BF16)
-        g_rows = grads_in[sources].reshape(count, grads_in.shape[2]).astype(BF16)
+        g_rows = grads_in[:, g].reshape(count, grads_in.shape[3]).astype(BF16)
         contract = (((0,), (0,)), ((), ()))
         total = lax.dot_general(
             jnp.concatenate([g_rows, g_rows, g_rows], axis=0),
@@ -278,9 +284,16 @@
         sums_out[:, :, pl.ds(pl.multiple_of(g * cols, cols), cols)] = total[:rank].reshape(
             STRIPES, rank // STRIPES, cols
         )
-        return carry
-
-    lax.fori_loop(0, n // GROUP, block, 0)
+
+    def rest(step, carry):
+        at = lax.rem(octet + step, flight) * STRIPES
+        spread(at)
+        block(lax.rem(octet + step - 1, flight))
+        finish(at)
+        return carry
+
+    lax.fori_loop(1, flight, rest, 0)
+    block(lax.rem(octet + flight - 1, flight))
 
     for step in range(1, STRIPES):
         target = lax.rem(member + step, STRIPES)
@@ -292,13 +305,13 @@
             device_id={"expert": base + target},
         ).start()
     sums_in[member] = sums_out[member]
-    others = pl.ds(0, STRIPES - 1)
     pltpu.make_async_copy(
         rows.at[:, pl.ds(0, n - 1)], rows.at[:, pl.ds(0, n - 1)], send_sem
     ).wait()
-    pltpu.make_async_copy(
-        grads_in.at[pl.ds(0, n - 1)], grads_in.at[pl.ds(0, n - 1)], gsend_sem
-    ).wait()
+    if flight > 1:
+        some = grads_out.at[pl.ds(0, flight - 1)]
+        pltpu.make_async_copy(some, some, gsend_sem.at[0]).wait()
+    pltpu.make_async_copy(grads_in.at[others], grads_in.at[others], gsend_sem.at[1]).wait()
     pltpu.make_async_copy(sums_in.at[others], sums_in.at[others], srecv_sem).wait()
     total = sums_in[0]
     for j in range(1, STRIPES):
@@ -313,7 +326,7 @@
     tok_rows, width = tokens.shape
     hidden_units = w_gate.shape[2]
     rank = out_proj.shape[1]
-    part = width // 2 // HALVES
+    part = width // 2 // PIECES
     out_cols = n * tok_rows // EX_LEN * rank
     rank_each = rank // STRIPES
     dma = pltpu.SemaphoreType.DMA
@@ -331,18 +344,18 @@
             pltpu.VMEM((width, hidden_units), BF16),
             pltpu.VMEM((rank, hidden_units), BF16),
             pltpu.VMEM((rank, width), BF16),
-            pltpu.VMEM((HALVES, flight, 2 * CAPACITY, part), BF16),
-            pltpu.VMEM((HALVES, n, 2 * CAPACITY, part), BF16),
+            pltpu.VMEM((PIECES, flight, 2 * CAPACITY, part), BF16),
+            pltpu.VMEM((PIECES, n, 2 * CAPACITY, part), BF16),
             pltpu.VMEM((flight, CAPACITY, 2 * rank), F32),
-            pltpu.VMEM((n, CAPACITY, 2 * rank), F32),
+            pltpu.VMEM((STRIPES, flight, CAPACITY, 2 * rank), F32),
             pltpu.VMEM((STRIPES, rank_each, out_cols), F32),
             pltpu.VMEM((STRIPES, rank_each, out_cols), F32),
             dma((8,)),
-            dma((HALVES,)),
+            dma((PIECES,)),
             dma,
-            dma((HALVES, n)),
-            dma,
-            dma,
+            dma((PIECES, n)),
+            dma((2,)),
+            dma((2,)),
             dma,
             dma,
         ],

time: 29.3 us -> 28.6 us (0.976)
  Pallas kernels: 27.7 us -> 27 us
    pallas_call x1, Pallas kernels: 27.7 us -> 27 us  [on_device(): pl.pallas_call(functools.partial(kernel, n), out_shape=jax.ShapeDtypeStru...]
where the time goes in v3:
time: 28.6 us; the launch traced here: 28.3 us
  Pallas kernels  27 us (94%)
  local copies, waits for them, and re-layouts  1.3 us (5%)
    pallas_call x1, Pallas kernels, on_device(): pl.pallas_call(functools.partial(kernel, n), out_shape=jax.ShapeDtypeStru...  27 us
    unnamed x1, local copies, waits for them, and re-layouts  1.3 us

profile of v3, /device:TPU:0, one launch (start us, length us, event | category | flops | bytes accessed | tf_op | source)
XLA Modules:
  0.0 28.3 jit_solution(5595392627822289197)
XLA Ops:
  0.0 27.0 %shard_map.82 = f32[8,256]{1,0:T(8,128)} custom-call(bf16[128,7168]{1,0:T(8,128)(2,1)} %tokens.1, bf16[128,7168]{1,0:T(8,128)(2,1)} %out_grad.1, s32[8,128]{1,0:T(8,128)} %bitcast.6, f32[8,128]{1,0:T(8,128)} %bitcast.7, bf16[1,7168,256]{2,1,0:T(8,128)(2,1)} %w_gate.1, bf16[1,7168,256]{2,1,0:T(8,128)(2,1)} %w_up.1, bf16[1,64,256]{2,1,0:T(8,128)(2,1)} %bitcast.5, ...), custom_call_target="tpu_custom_call" | custom-call | tf_op jit(solution)/shard_map/pallas_call | solution.py:333
  27.0 1.3 %copy.10 = f32[8,256]{1,0:T(8,128)} copy(f32[8,256]{1,0:T(8,128)} %shard_map.82) | data formatting | bytes 16384

commit v4 on v3

--- a/solution.py
+++ b/solution.py
@@ -11,7 +11,8 @@
 CAPACITY = 8
 PIECES = 2
 ORDER = (1, 0)
-DIAGONAL_BY_FAR = (0,)
+BY_FAR_FIRST = ()
+BY_FAR_LATER = (0,)
 BF16 = jnp.bfloat16
 F32 = jnp.float32
 BY_LAST = (((1,), (1,)), ((), ()))
@@ -196,15 +197,15 @@
                 device_id={"expert": base + lax.rem(member + step, STRIPES)},
             ).start()
 
-    def spread(at):
+    def spread(at, by_far):
         near_source, far_source = at + toggled(member, 1), at + toggled(member, 2)
         for h in ORDER:
             arrived(far_source, h)
-            if h not in DIAGONAL_BY_FAR:
+            if h not in by_far:
                 send(rows.at[h, far_source], far_source, h, near)
             send(rows.at[h, far_source], far_source, h, core)
             arrived(near_source, h)
-            if h in DIAGONAL_BY_FAR:
+            if h in by_far:
                 send(rows.at[h, near_source], near_source, h, far)
             send(rows.at[h, near_source], near_source, h, core)
 
@@ -214,15 +215,14 @@
             arrived(diagonal, h)
             send(rows.at[h, diagonal], diagonal, h, core)
 
-    def settle(at):
+    def settle(at, h):
         for bits in ((), (1,), (2,), (1, 2)):
             source = toggled(member, 0)
             for bit in bits:
                 source = toggled(source, bit)
-            for h in range(PIECES):
-                arrived(at + source, h)
-
-    spread(base)
+            arrived(at + source, h)
+
+    spread(base, BY_FAR_FIRST)
 
     def onward(step, carry):
         at = lax.rem(octet + step, flight) * STRIPES
@@ -254,11 +254,11 @@
     ) == lax.div(lax.broadcasted_iota(jnp.int32, (count, cols), 1), rank)
 
     def block(g):
-        settle(g * STRIPES)
         sources = pl.ds(pl.multiple_of(g * STRIPES, STRIPES), STRIPES)
         gate = jnp.zeros((count, wg.shape[1]), F32)
         up = jnp.zeros((count, wg.shape[1]), F32)
-        for h in range(PIECES):
+        for h in ORDER:
+            settle(g * STRIPES, h)
             both = rows[h, sources].astype(F32)
             for side in range(2):
                 x = both[:, side * CAPACITY : (side + 1) * CAPACITY].reshape(count, part)
@@ -287,7 +287,7 @@
 
     def rest(step, carry):
         at = lax.rem(octet + step, flight) * STRIPES
-        spread(at)
+        spread(at, BY_FAR_LATER)
         block(lax.rem(octet + step - 1, flight))
         finish(at)
         return carry

time: 28.6 us -> 28.1 us (0.983)
  Pallas kernels: 27 us -> 26.6 us
    pallas_call x1, Pallas kernels: 27 us -> 26.6 us  [on_device(): pl.pallas_call(functools.partial(kernel, n), out_shape=jax.ShapeDtypeStru...]
where the time goes in v4:
time: 28.1 us; the launch traced here: 27.9 us
  Pallas kernels  26.6 us (95%)
  local copies, waits for them, and re-layouts  1.3 us (5%)
    pallas_call x1, Pallas kernels, on_device(): pl.pallas_call(functools.partial(kernel, n), out_shape=jax.ShapeDtypeStru...  26.6 us
    unnamed x1, local copies, waits for them, and re-layouts  1.3 us

profile of v4, /device:TPU:0, one launch (start us, length us, event | category | flops | bytes accessed | tf_op | source)
XLA Modules:
  0.0 27.9 jit_solution(17741089912768973360)
XLA Ops:
  0.0 26.6 %shard_map.82 = f32[8,256]{1,0:T(8,128)} custom-call(bf16[128,7168]{1,0:T(8,128)(2,1)} %tokens.1, bf16[128,7168]{1,0:T(8,128)(2,1)} %out_grad.1, s32[8,128]{1,0:T(8,128)} %bitcast.6, f32[8,128]{1,0:T(8,128)} %bitcast.7, bf16[1,7168,256]{2,1,0:T(8,128)(2,1)} %w_gate.1, bf16[1,7168,256]{2,1,0:T(8,128)(2,1)} %w_up.1, bf16[1,64,256]{2,1,0:T(8,128)(2,1)} %bitcast.5, ...), custom_call_target="tpu_custom_call" | custom-call | tf_op jit(solution)/shard_map/pallas_call | solution.py:333
  26.6 1.3 %copy.10 = f32[8,256]{1,0:T(8,128)} copy(f32[8,256]{1,0:T(8,128)} %shard_map.82) | data formatting | bytes 16384

commit v5 on v4

--- a/solution.py
+++ b/solution.py
@@ -120,14 +120,6 @@
 
     loads[2].wait()
     half = width // 2
-    for h in range(PIECES):
-        lo = h * part
-        left = jnp.dot(sel, tok[:, lo : lo + part], preferred_element_type=F32)
-        right = jnp.dot(sel, tok[:, half + lo : half + lo + part], preferred_element_type=F32)
-        for e in range(flight):
-            at = slice(e * CAPACITY, (e + 1) * CAPACITY)
-            outgoing[h, e] = jnp.concatenate([left[at], right[at]], axis=0).astype(BF16)
-
     pl.semaphore_wait(barrier, flight - 1 + STRIPES - 1)
 
     def send(src, source, h, target):
@@ -146,15 +138,21 @@
 
     core, near, far = (base + toggled(member, bit) for bit in range(3))
 
-    def across(step, carry):
-        e = lax.rem(octet + step, flight)
-        for h in ORDER:
-            send(outgoing.at[h, e], me, h, e * STRIPES + member)
-        return carry
-
-    lax.fori_loop(1, flight, across, 0)
     own = []
     for h in ORDER:
+        lo = h * part
+        left = jnp.dot(sel, tok[:, lo : lo + part], preferred_element_type=F32)
+        right = jnp.dot(sel, tok[:, half + lo : half + lo + part], preferred_element_type=F32)
+        for e in range(flight):
+            at = slice(e * CAPACITY, (e + 1) * CAPACITY)
+            outgoing[h, e] = jnp.concatenate([left[at], right[at]], axis=0).astype(BF16)
+
+        def across(step, carry):
+            e = lax.rem(octet + step, flight)
+            send(outgoing.at[h, e], me, h, e * STRIPES + member)
+            return carry
+
+        lax.fori_loop(1, flight, across, 0)
         for target in (far, near, core):
             send(outgoing.at[h, octet], me, h, target)
         keep = pltpu.make_async_copy(outgoing.at[h, octet], rows.at[h, me], local_sem.at[h])

time: 28.1 us -> 27.9 us (level)
  no operation moved by 1% of the time
where the time goes in v5:
time: 27.9 us; the launch traced here: 27.7 us
  Pallas kernels  26.4 us (95%)
  local copies, waits for them, and re-layouts  1.3 us (5%)
    pallas_call x1, Pallas kernels, on_device(): pl.pallas_call(functools.partial(kernel, n), out_shape=jax.ShapeDtypeStru...  26.4 us
    unnamed x1, local copies, waits for them, and re-layouts  1.3 us

profile of v5, /device:TPU:0, one launch (start us, length us, event | category | flops | bytes accessed | tf_op | source)
XLA Modules:
  0.0 27.7 jit_solution(1157470949871822572)
XLA Ops:
  0.0 26.4 %shard_map.82 = f32[8,256]{1,0:T(8,128)} custom-call(bf16[128,7168]{1,0:T(8,128)(2,1)} %tokens.1, bf16[128,7168]{1,0:T(8,128)(2,1)} %out_grad.1, s32[8,128]{1,0:T(8,128)} %bitcast.6, f32[8,128]{1,0:T(8,128)} %bitcast.7, bf16[1,7168,256]{2,1,0:T(8,128)(2,1)} %w_gate.1, bf16[1,7168,256]{2,1,0:T(8,128)(2,1)} %w_up.1, bf16[1,64,256]{2,1,0:T(8,128)(2,1)} %bitcast.5, ...), custom_call_target="tpu_custom_call" | custom-call | tf_op jit(solution)/shard_map/pallas_call | solution.py:331
  26.4 1.3 %copy.10 = f32[8,256]{1,0:T(8,128)} copy(f32[8,256]{1,0:T(8,128)} %shard_map.82) | data formatting | bytes 16384
